TPU v7x, 128 devices: a whole 4x4x4 slice. The times are simulated.
128 devices in a mesh: var: 8 (over x, y_lo), space: 16 (over z, y_hi, core).
Axes of the slice: x: 4, y: 4 (y_hi: 2, y_lo: 2; y = y_hi * 2 + y_lo), z: 4, core: 2. Of those that a mesh axis runs over, the one named last changes fastest.
Arguments:
- pixels: bfloat16 [64, 1024, 4096], P('var', 'space'), may hold values from -6 to 6
- counts: int32 [64, 64, 256], P('var', 'space'), may hold values from 0 to 256
- embed_weight: bfloat16 [64, 32, 32, 512], P('var'), may hold values from -0.1875 to 0.1875
- var_embed: bfloat16 [64, 512], P('var'), may hold values from -3 to 3
- query: float32 [512], replicated, may hold values from -140 to 140
- key_weight: bfloat16 [512, 512], replicated, may hold values from -0.25 to 0.25
- value_weight: bfloat16 [512, 512], replicated, may hold values from -0.25 to 0.25
- out_weight: bfloat16 [512, 512], replicated, may hold values from -0.25 to 0.25
Outputs:
- aggregated: bfloat16 [64, 256, 512], P('space', 'var')
All inputs are finite; a program needn't handle non-finite values.
Results may differ from a plain program's by a relative error of at most 0.011.
Values may be sent and summed in bfloat16 or wider, within the bound.
No kernel may reach another device: no remote copies, remote signals or barrier semaphores. Data moves between devices by JAX's collectives and lax.ppermute only.
A program may use at most 128 MiB of HBM per device.

v0:
```python
import functools
import math

import jax
import jax.numpy as jnp
from jax import lax
from jax.experimental import pallas as pl
from jax.experimental.pallas import tpu as pltpu
from jax.sharding import PartitionSpec as P

HEADS = 8
HEAD = 64
PATCH = 16
D = 512
COLS = 4096
PC = 256
LANES = 128
TILES = COLS // LANES
VPD = 8
DEVS = 8
OWN = PC // DEVS
BF = jnp.bfloat16
F32 = jnp.float32
NT = (((1,), (1,)), ((), ()))


def three_parts(x):
    high = x.astype(BF)
    rest = x - high.astype(F32)
    middle = rest.astype(BF)
    return high, middle, (rest - middle.astype(F32)).astype(BF)


def relayout_group(rows, stage, edge_stage, out):
    for t in range(TILES):
        stage[t * 8 : t * 8 + 8, :] = rows[:, t * LANES : (t + 1) * LANES]
    skewed = [
        pltpu.roll(stage[pl.ds(r, TILES, stride=8), :].astype(BF), (16 * r + 8) % LANES, 1) for r in range(8)
    ]
    lane = lax.broadcasted_iota(jnp.int32, (TILES, LANES), 1)
    level = [skewed[(-k) % 8] for k in range(8)]
    for bit in (1, 2, 4):
        chosen = ((lane // 16) & bit) != 0
        level = [jnp.where(chosen, level[(k - bit) % 8], level[k]) for k in range(8)]
    for k in range(1, 8):
        out[k * TILES : (k + 1) * TILES, :] = pltpu.roll(level[k], (-16 * k) % LANES, 1)
    edge_stage[8 : 8 + TILES, :] = level[0].astype(F32)
    left = (lane % 16) < 8
    out[0:TILES, :] = jnp.where(left, edge_stage[7 : 7 + TILES, :].astype(BF), level[0])
    out[8 * TILES : 9 * TILES, :] = jnp.where(left, level[0], edge_stage[9 : 9 + TILES, :].astype(BF))


def permutation():
    row = lax.broadcasted_iota(jnp.int32, (PC, PC), 0)
    col = lax.broadcasted_iota(jnp.int32, (PC, PC), 1)
    same = ((row // 8) == (col % TILES)) & ((row % 8) == (col // TILES))
    return jnp.where(same, 1.0, 0.0).astype(BF)


def embed_kernel(edge, *refs):
    if edge:
        low_hbm, high_hbm, ext_hbm, *refs = refs
    else:
        query_ref, key_hbm, value_hbm, *refs = refs
    px_hbm, w_hbm, cnt_ref, ve_ref, msg_ref, *refs = refs
    if not edge:
        ext_out, *refs = refs
    (px, w, ext, a_even, a_odd, stage_even, stage_odd, edges, bias_ref, off_ref, top_ref, tot_ref, acc_ref, px_sem, w_sem,
     *more) = refs
    if not edge:
        key_ref, value_ref = more[1:]
    rows = (0, 3) if edge else (1, 2)
    starts = (0, 4) if edge else (0, 2)

    def px_copies(v):
        copies = [pltpu.make_async_copy(px_hbm.at[v], px.at[v], px_sem.at[v])]
        if edge:
            low, high, halo_sem, _ = more
            copies.append(pltpu.make_async_copy(low_hbm.at[v], low.at[v], halo_sem.at[0, v]))
            copies.append(pltpu.make_async_copy(high_hbm.at[v], high.at[v], halo_sem.at[1, v]))
        return copies

    def w_copy(v):
        return pltpu.make_async_copy(w_hbm.at[v], w.at[v], w_sem.at[v])

    def fetch(v):
        for copy in px_copies(v):
            copy.start()
        w_copy(v).start()

    for copy in px_copies(0):
        copy.start()
    if edge:
        first_copies = [pltpu.make_async_copy(ext_hbm, ext, more[3].at[0])]
    else:
        first_copies = [
            pltpu.make_async_copy(key_hbm, key_ref, more[0].at[0]),
            pltpu.make_async_copy(value_hbm, value_ref, more[0].at[1]),
        ]
    for copy in first_copies:
        copy.start()
    w_copy(0).start()
    fetch(1)
    for copy in px_copies(2):
        copy.start()

    def relayout(v, a_ref, stage):
        body = px[v].astype(F32)
        if edge:
            groups = [more[0][v].astype(F32), body[0:8], body[8:16], body[16:24],
                      body[40:48], body[48:56], body[56:64], more[1][v].astype(F32)]
        else:
            groups = [body[8 * n : 8 * n + 8] for n in range(1, 7)]
        for n, group in enumerate(groups):
            relayout_group(group, stage.at[n], edges.at[n], a_ref.at[n])

    def compute(v, a_ref):
        a = jnp.concatenate(
            [
                jnp.concatenate([a_ref[start + g, b * TILES : b * TILES + PC, :] for g in range(4) for b in range(2)], 1)
                for start in starts
            ],
            0,
        )
        weight = jnp.concatenate(
            [w[v, 8 * g : 8 * g + 8, 16 * b : 16 * b + 16, :].reshape(LANES, D) for g in range(4) for b in range(2)], 0
        )
        tokens = (jnp.dot(a, weight, preferred_element_type=F32) + off_ref[v]).astype(BF)
        both = lax.dot_general(ext[...], tokens, NT, preferred_element_type=F32)
        scores = both[D : D + 8] + both[D + 8 : D + 16] + both[D + 16 : D + 24] + bias_ref[v]
        old = top_ref[...]
        top = jnp.maximum(old, scores)
        decay = jnp.exp(old - top)
        fresh = jnp.exp(scores - top)
        top_ref[...] = top
        tot_ref[...] = tot_ref[...] * decay + fresh
        for h in range(HEADS):
            at = slice(h * HEAD, (h + 1) * HEAD)
            acc_ref[at, :] = acc_ref[at, :] * decay[h : h + 1] + both[at] * fresh[h : h + 1]

    edges[...] = jnp.zeros_like(edges)
    perm = permutation()
    valid = jnp.concatenate([cnt_ref[v].astype(F32) for v in range(VPD)], 0).astype(BF)
    bias = jnp.log((1.0 + jnp.dot(valid, perm, preferred_element_type=F32)) / (1.0 + PATCH * PATCH))
    offsets = ve_ref[...].astype(F32)
    for v in range(VPD):
        off_ref[v] = offsets[v : v + 1]
        bias_ref[v] = jnp.concatenate([bias[4 * v + row : 4 * v + row + 1] for row in rows], 1)
    top_ref[...] = jnp.full_like(top_ref, -1e30)
    tot_ref[...] = jnp.zeros_like(tot_ref)
    acc_ref[...] = jnp.zeros_like(acc_ref)
    for copy in first_copies:
        copy.wait()
    if not edge:
        head = lax.broadcasted_iota(jnp.int32, (HEADS, D), 0)
        col = lax.broadcasted_iota(jnp.int32, (HEADS, D), 1)
        spread = jnp.where(col // HEAD == head, jnp.broadcast_to(query_ref[...], (HEADS, D)), 0.0)
        parts = lax.dot_general(jnp.concatenate(three_parts(spread), 0), key_ref[...], NT, preferred_element_type=F32)
        kq = (parts[0:8] + parts[8:16] + parts[16:24]) / math.sqrt(HEAD)
        ext[0:D, :] = value_ref[...].T
        ext[D : D + 32, :] = jnp.concatenate((*three_parts(kq), jnp.zeros((8, D), BF)), 0)
        ext_out[...] = ext[...]
    for copy in px_copies(0):
        copy.wait()
    relayout(0, a_even, stage_even)

    def pair(step, _):
        even = 2 * step
        later = jnp.minimum(even + 2, VPD - 1)

        @pl.when(step < VPD // 2 - 1)
        def _():
            w_copy(even + 2).start()
            fetch(even + 3)

        @pl.when(step < VPD // 2 - 2)
        def _():
            for copy in px_copies(even + 4):
                copy.start()

        w_copy(even).wait()
        w_copy(even + 1).wait()
        for copy in px_copies(even + 1):
            copy.wait()

        @pl.when(step < VPD // 2 - 1)
        def _():
            for copy in px_copies(even + 2):
                copy.wait()

        relayout(even + 1, a_odd, stage_odd)
        compute(even, a_even)
        relayout(later, a_even, stage_even)
        compute(even + 1, a_odd)
        return 0

    lax.fori_loop(0, VPD // 2, pair, 0)

    lane = lax.broadcasted_iota(jnp.int32, (24, LANES), 1)
    total = tot_ref[...]
    parts = jnp.concatenate(three_parts(top_ref[...] + jnp.log(total)), 0)
    sums = []
    for n in range(2):
        half = slice(n * PC, (n + 1) * PC)
        weighted = jnp.concatenate(
            [acc_ref[h * HEAD : (h + 1) * HEAD, half] / total[h : h + 1, half] for h in range(HEADS)], 0
        ).astype(BF)
        natural = lax.dot_general(perm, weighted, NT, preferred_element_type=F32).astype(BF)
        for d in range(DEVS):
            msg_ref[d, n * OWN : (n + 1) * OWN, :] = natural[d * OWN : (d + 1) * OWN]
        sums.append(lax.dot_general(parts[:, half], perm, NT, preferred_element_type=F32))
    for d in range(DEVS):
        spot = d * OWN // LANES * LANES
        picked = jnp.zeros((24, LANES), F32)
        for n in range(2):
            moved = pltpu.roll(sums[n][:, spot : spot + LANES], (n * OWN - d * OWN) % LANES, 1)
            picked = jnp.where(lane // OWN == n, moved, picked)
        wide = jnp.concatenate([picked[0:8], picked[8:16], picked[16:24], jnp.zeros((8, LANES), F32)], 1)
        msg_ref[d, 2 * OWN : 2 * OWN + 16, :] = jnp.concatenate([wide, jnp.zeros((8, D), F32)], 0).astype(BF)


def embed(edge, extras, pixels, weight, counts, var_embed):
    groups = 8 if edge else 6
    hbm = pl.BlockSpec(memory_space=pl.ANY)
    vmem = pl.BlockSpec(memory_space=pltpu.VMEM)
    out_shape = [jax.ShapeDtypeStruct((DEVS, 2 * OWN + 16, D), BF)]
    scratch = [
        pltpu.VMEM((VPD, 64, COLS), BF),
        pltpu.VMEM((VPD, 32, 32, D), BF),
        pltpu.VMEM((D + 32, D), BF),
        pltpu.VMEM((groups, PC + TILES, LANES), BF),
        pltpu.VMEM((groups, PC + TILES, LANES), BF),
        pltpu.VMEM((groups, TILES * 8, LANES), F32),
        pltpu.VMEM((groups, TILES * 8, LANES), F32),
        pltpu.VMEM((groups, TILES + 16, LANES), F32),
        pltpu.VMEM((VPD, 1, 2 * PC), F32),
        pltpu.VMEM((VPD, 1, D), F32),
        pltpu.VMEM((HEADS, 2 * PC), F32),
        pltpu.VMEM((HEADS, 2 * PC), F32),
        pltpu.VMEM((D, 2 * PC), F32),
        pltpu.SemaphoreType.DMA((VPD,)),
        pltpu.SemaphoreType.DMA((VPD,)),
    ]
    if edge:
        scratch += [
            pltpu.VMEM((VPD, 8, COLS), BF),
            pltpu.VMEM((VPD, 8, COLS), BF),
            pltpu.SemaphoreType.DMA((2, VPD)),
            pltpu.SemaphoreType.DMA((1,)),
        ]
    else:
        scratch += [pltpu.SemaphoreType.DMA((2,)), pltpu.VMEM((D, D), BF), pltpu.VMEM((D, D), BF)]
        out_shape.append(jax.ShapeDtypeStruct((D + 32, D), BF))
    return pl.pallas_call(
        functools.partial(embed_kernel, edge),
        in_specs=[hbm if edge else vmem, hbm, hbm, hbm, hbm, vmem, vmem],
        out_specs=[vmem] * len(out_shape),
        out_shape=out_shape,
        scratch_shapes=scratch,
        compiler_params=pltpu.CompilerParams(vmem_limit_bytes=56 * 2**20),
        cost_estimate=pl.CostEstimate(flops=8 * 2 * 512 * (1024 + 512) * 512, bytes_accessed=13 * 2**20, transcendentals=0),
        name="embed_edge" if edge else "embed_inner",
    )(*extras, pixels, weight, counts, var_embed)


def finish_kernel(inner_ref, outer_ref, wo_ref, out_ref):
    head = lax.broadcasted_iota(jnp.int32, (HEADS, D), 0)
    col = lax.broadcasted_iota(jnp.int32, (HEADS, D), 1)
    one = jnp.where(col // HEAD == head, 1.0, 0.0).astype(BF)
    spread = jnp.concatenate((one, one), 0)
    for ref, rows in ((inner_ref, (1, 2)), (outer_ref, (0, 3))):
        sums = []
        for s in range(DEVS):
            wide = ref[s, 2 * OWN : 2 * OWN + 16, :].astype(F32)[0:8]
            sums.append(wide[:, 0:LANES] + wide[:, LANES : 2 * LANES] + wide[:, 2 * LANES : 3 * LANES])
        top = functools.reduce(jnp.maximum, sums)
        parts = [jnp.exp(x - top) for x in sums]
        scale = 1.0 / functools.reduce(jnp.add, parts)
        mixture = jnp.zeros((2 * OWN, D), F32)
        for s in range(DEVS):
            share = parts[s] * scale
            high = share.astype(BF)
            low = (share - high.astype(F32)).astype(BF)
            wide = lax.dot_general(jnp.concatenate((high, low), 0), spread, (((0,), (0,)), ((), ())), preferred_element_type=F32)
            mixture = mixture + wide[0 : 2 * OWN] * ref[s, 0 : 2 * OWN, :].astype(F32)
        result = jnp.dot(mixture.astype(BF), wo_ref[...], preferred_element_type=F32).astype(BF)
        for n, row in enumerate(rows):
            out_ref[row] = result[n * OWN : (n + 1) * OWN]


def finish(inner, outer, out_weight):
    return pl.pallas_call(
        finish_kernel,
        out_shape=jax.ShapeDtypeStruct((4, OWN, D), BF),
        compiler_params=pltpu.CompilerParams(vmem_limit_bytes=24 * 2**20),
        name="finish",
    )(inner, outer, out_weight)


def exchange(msg):
    return lax.all_to_all(msg, "var", 0, 0)


def shards(pixels, counts, embed_weight, var_embed, query, key_weight, value_weight, out_weight):
    count = lax.axis_size("space")
    forward = [(i, i + 1) for i in range(count - 1)]
    low = lax.ppermute(pixels[:, 56:64], "space", forward)
    high = lax.ppermute(pixels[:, 0:8], "space", [(b, a) for a, b in forward])
    rest = (pixels, embed_weight, counts, var_embed)
    inner, ext = embed(False, (query.reshape(1, D), key_weight, value_weight), *rest)
    inner = exchange(inner)
    (outer,) = embed(True, (low, high, ext), *rest)
    outer = exchange(outer)
    return finish(inner, outer, out_weight)


def solution(mesh):
    return jax.shard_map(
        shards,
        mesh=mesh,
        in_specs=(
            P("var", "space", None),
            P("var", "space", None),
            P("var", None, None, None),
            P("var", None),
            P(),
            P(),
            P(),
            P(),
        ),
        out_specs=P("space", "var", None),
        check_vma=False,
    )
```

profile of v0, /device:TPU:96, one launch (start us, length us, event | category | flops | bytes accessed | tf_op | source)
XLA Modules:
  0.0 61.1 jit_solution(17645268997605629178)
XLA Ops:
  0.0 1.3 %fusion = (bf16[8,8,4096]{2,1,0:T(8,128)(2,1)S(1)}, bf16[8,8,4096]{2,1,0:T(8,128)(2,1)S(1)}) fusion(bf16[8,64,4096]{2,1,0:T(8,128)(2,1)} %refs_3_.3), kind=kLoop, calls=%fused_computation | loop fusion | bytes 2097152 | tf_op jit(solution)/shard_map/slice | solution.py:308
  1.3 1.9 %collective-permute-start = (bf16[8,8,4096]{2,1,0:T(8,128)(2,1)S(1)}, bf16[8,8,4096]{2,1,0:T(8,128)(2,1)S(1)}, u32[]{:S(2)}, u32[]{:S(2)}) collective-permute-start(bf16[8,8,4096]{2,1,0:T(8,128)(2,1)S(1)} %get-tuple-element.10), channel_id=1, source_target_pairs={{0,1},{1,2},{2,3},{3,4},{4,5},{5,6},{6,7},{7,8},{8,9},{9,10},{10,1... | collective-permute-start | bytes 1572872 | tf_op jit(solution)/shard_map/ppermute | solution.py:307
  3.2 6.0 %collective-permute-start.1 = (bf16[8,8,4096]{2,1,0:T(8,128)(2,1)S(1)}, bf16[8,8,4096]{2,1,0:T(8,128)(2,1)S(1)}, u32[]{:S(2)}, u32[]{:S(2)}) collective-permute-start(bf16[8,8,4096]{2,1,0:T(8,128)(2,1)S(1)} %get-tuple-element.9), channel_id=1, source_target_pairs={{1,0},{2,1},{3,2},{4,3},{5,4},{6,5},{7,6},{8,7},{9,8},{10,9},{11,1... | collective-permute-start | bytes 1572872 | tf_op jit(solution)/shard_map/ppermute | solution.py:308
  9.3 14.3 %embed_inner.1 = (bf16[8,80,512]{2,1,0:T(8,128)(2,1)}, bf16[544,512]{1,0:T(8,128)(2,1)}) custom-call(f32[1,512]{1,0:T(1,128)} %bitcast.1, bf16[512,512]{1,0:T(8,128)(2,1)} %refs_1_.1, bf16[512,512]{1,0:T(8,128)(2,1)} %refs_2_.1, bf16[8,64,4096]{2,1,0:T(8,128)(2,1)} %refs_3_.3, bf16[8,32,32,512]{3,2,1,0:T(8,128)(2,1)} %refs_4_.3, s32[8,4,256]{2,1,0:T(4,128)} %refs_5_.3, ...), custom_call_target="tpu_custom_call" | custom-call | flops 6442450944 | bytes 13631488 | tf_op jit(solution)/shard_map/embed_inner/pallas_call | solution.py:254
  23.6 5.3 %all-to-all-start = ((bf16[8,80,512]{2,1,0:T(8,128)(2,1)}), bf16[8,80,512]{2,1,0:T(8,128)(2,1)S(1)}, u32[]{:S(2)}, u32[]{:S(2)}) async-start(bf16[8,80,512]{2,1,0:T(8,128)(2,1)} %get-tuple-element.7), calls=%async_computation | async-start | bytes 1310720 | tf_op jit(solution)/shard_map/all_to_all | solution.py:301
  28.9 0.0 collective-permute-done.refs_0_
  28.9 0.0 copy-start.1
  28.9 0.0 collective-permute-done.1.refs_1_
  28.9 0.0 copy-start.2
  29.0 0.8 %copy-done.1 = bf16[8,8,4096]{2,1,0:T(8,128)(2,1)} copy-done((bf16[8,8,4096]{2,1,0:T(8,128)(2,1)}, bf16[8,8,4096]{2,1,0:T(8,128)(2,1)S(1)}, u32[]{:S(2)}) %copy-start.1) | copy-done | bytes 524312
  29.7 0.2 copy-done.2
  29.9 0.0 copy-start
  29.9 14.3 %embed_edge.1 = bf16[8,80,512]{2,1,0:T(8,128)(2,1)} custom-call(bf16[8,8,4096]{2,1,0:T(8,128)(2,1)} %copy-done.1, bf16[8,8,4096]{2,1,0:T(8,128)(2,1)} %copy-done.2, bf16[544,512]{1,0:T(8,128)(2,1)} %get-tuple-element.8.refs_2_, bf16[8,64,4096]{2,1,0:T(8,128)(2,1)} %refs_3_.3, bf16[8,32,32,512]{3,2,1,0:T(8,128)(2,1)} %refs_4_.3, s32[8,4,256]{2,1,0:T(4,128)} %refs_5_.3, ...), custom_call_target="tpu_custom_call" | custom-call | flops 6442450944 | bytes 13631488 | tf_op jit(solution)/shard_map/embed_edge/pallas_call | solution.py:254
  44.2 0.0 all-to-all-done.inner_ref
  44.3 15.1 %all_to_all.10.outer_ref = bf16[8,80,512]{2,1,0:T(8,128)(2,1)S(1)} all-to-all(bf16[8,80,512]{2,1,0:T(8,128)(2,1)} %embed_edge.1), channel_id=1, replica_groups=mesh['var'=8,'space'=16] {'var'}, dimensions={0} | all-to-all | bytes 1310720 | tf_op jit(solution)/shard_map/all_to_all | solution.py:301
  59.4 0.0 copy-done
  59.4 1.7 %finish.1 = bf16[4,32,512]{2,1,0:T(8,128)(2,1)} custom-call(bf16[8,80,512]{2,1,0:T(8,128)(2,1)S(1)} %all-to-all-done.inner_ref, bf16[8,80,512]{2,1,0:T(8,128)(2,1)S(1)} %all_to_all.10.outer_ref, bf16[512,512]{1,0:T(8,128)(2,1)S(1)} %copy-done), custom_call_target="tpu_custom_call" | custom-call | tf_op jit(solution)/shard_map/finish/pallas_call | solution.py:292
Async XLA Ops:
  1.3 27.7 %collective-permute-start = (bf16[8,8,4096]{2,1,0:T(8,128)(2,1)S(1)}, bf16[8,8,4096]{2,1,0:T(8,128)(2,1)S(1)}, u32[]{:S(2)}, u32[]{:S(2)}) collective-permute-start(bf16[8,8,4096]{2,1,0:T(8,128)(2,1)S(1)} %get-tuple-element.10), channel_id=1, source_target_pairs={{0,1},{1,2},{2,3},{3,4},{4,5},{5,6},{6,7},{7,8},{8,9},{9,10},{10,1... | collective-permute-start | bytes 1572872 | tf_op jit(solution)/shard_map/ppermute | solution.py:307
  3.2 25.7 %collective-permute-start.1 = (bf16[8,8,4096]{2,1,0:T(8,128)(2,1)S(1)}, bf16[8,8,4096]{2,1,0:T(8,128)(2,1)S(1)}, u32[]{:S(2)}, u32[]{:S(2)}) collective-permute-start(bf16[8,8,4096]{2,1,0:T(8,128)(2,1)S(1)} %get-tuple-element.9), channel_id=1, source_target_pairs={{1,0},{2,1},{3,2},{4,3},{5,4},{6,5},{7,6},{8,7},{9,8},{10,9},{11,1... | collective-permute-start | bytes 1572872 | tf_op jit(solution)/shard_map/ppermute | solution.py:308
  23.6 20.7 %all-to-all-start = ((bf16[8,80,512]{2,1,0:T(8,128)(2,1)}), bf16[8,80,512]{2,1,0:T(8,128)(2,1)S(1)}, u32[]{:S(2)}, u32[]{:S(2)}) async-start(bf16[8,80,512]{2,1,0:T(8,128)(2,1)} %get-tuple-element.7), calls=%async_computation | async-start | bytes 1310720 | tf_op jit(solution)/shard_map/all_to_all | solution.py:301
  28.9 0.8 %copy-start.1 = (bf16[8,8,4096]{2,1,0:T(8,128)(2,1)}, bf16[8,8,4096]{2,1,0:T(8,128)(2,1)S(1)}, u32[]{:S(2)}) copy-start(bf16[8,8,4096]{2,1,0:T(8,128)(2,1)S(1)} %collective-permute-done.refs_0_) | copy-start | bytes 1572868
  28.9 1.0 %copy-start.2 = (bf16[8,8,4096]{2,1,0:T(8,128)(2,1)}, bf16[8,8,4096]{2,1,0:T(8,128)(2,1)S(1)}, u32[]{:S(2)}) copy-start(bf16[8,8,4096]{2,1,0:T(8,128)(2,1)S(1)} %collective-permute-done.1.refs_1_) | copy-start | bytes 1572868
  29.9 29.5 %copy-start = (bf16[512,512]{1,0:T(8,128)(2,1)S(1)}, bf16[512,512]{1,0:T(8,128)(2,1)}, u32[]{:S(2)}) copy-start(bf16[512,512]{1,0:T(8,128)(2,1)} %wo_ref.1) | copy-start | bytes 1572868
where the time goes:
time: 61.5 us; the launch traced here: 61.1 us
  Pallas kernels  30.4 us (49%)
  blocking collectives  15.1 us (25%)
  starting transfers between devices  13.3 us (22%)
  local copies, waits for them, and re-layouts  2.22 us (4%)
    pallas_call x2, Pallas kernels, embed(): pl.pallas_call(functools.partial(embed_kernel, edge), in_specs=[hbm if ed...  28.7 us
    all_to_all x1, blocking collectives, exchange(): return lax.all_to_all(msg, 'var', 0, 0)  15.1 us
    ppermute x1, starting transfers between devices, shards(): high = lax.ppermute(pixels[:, 0:8], 'space', [(b, a) for a, b in forward])  6.05 us
    all_to_all x1, starting transfers between devices, exchange(): return lax.all_to_all(msg, 'var', 0, 0)  5.34 us
    ppermute x1, starting transfers between devices, shards(): low = lax.ppermute(pixels[:, 56:64], 'space', forward)  1.92 us
    pallas_call x1, Pallas kernels, finish(): pl.pallas_call(finish_kernel, out_shape=jax.ShapeDtypeStruct((4, OWN, D),...  1.74 us
    slice x1, local copies, waits for them, and re-layouts, shards(): high = lax.ppermute(pixels[:, 0:8], 'space', [(b, a) for a, b in forward])  1.27 us
  transfers between devices with their start and end apart: 3, of which 0 were waited for; matrix products, arithmetic and copies ran while one was open for 0% of the time, Pallas kernels for 47%

commit v1 on v0

--- a/solution.py
+++ b/solution.py
@@ -59,62 +59,49 @@
 
 def embed_kernel(edge, *refs):
     if edge:
-        low_hbm, high_hbm, ext_hbm, *refs = refs
+        low_ref, high_ref, ext_hbm, *refs = refs
     else:
-        query_ref, key_hbm, value_hbm, *refs = refs
-    px_hbm, w_hbm, cnt_ref, ve_ref, msg_ref, *refs = refs
+        query_hbm, key_hbm, value_hbm, *refs = refs
+    px_hbm, w_hbm, cnt_hbm, ve_hbm, msg_ref, *refs = refs
     if not edge:
         ext_out, *refs = refs
-    (px, w, ext, a_even, a_odd, stage_even, stage_odd, edges, bias_ref, off_ref, top_ref, tot_ref, acc_ref, px_sem, w_sem,
-     *more) = refs
-    if not edge:
-        key_ref, value_ref = more[1:]
+    (px, w, ext, cnt_ref, ve_ref, a_even, a_odd, stage_even, stage_odd, edges, tok_even, tok_odd, bias_ref, off_ref,
+     top_ref, tot_ref, acc_ref, px_sem, w_sem, sem, *more) = refs
     rows = (0, 3) if edge else (1, 2)
     starts = (0, 4) if edge else (0, 2)
 
-    def px_copies(v):
-        copies = [pltpu.make_async_copy(px_hbm.at[v], px.at[v], px_sem.at[v])]
-        if edge:
-            low, high, halo_sem, _ = more
-            copies.append(pltpu.make_async_copy(low_hbm.at[v], low.at[v], halo_sem.at[0, v]))
-            copies.append(pltpu.make_async_copy(high_hbm.at[v], high.at[v], halo_sem.at[1, v]))
-        return copies
+    def px_copy(v):
+        return pltpu.make_async_copy(px_hbm.at[v], px.at[v], px_sem.at[v])
 
     def w_copy(v):
         return pltpu.make_async_copy(w_hbm.at[v], w.at[v], w_sem.at[v])
 
-    def fetch(v):
-        for copy in px_copies(v):
-            copy.start()
-        w_copy(v).start()
-
-    for copy in px_copies(0):
-        copy.start()
+    small = [(cnt_hbm, cnt_ref), (ve_hbm, ve_ref)]
     if edge:
-        first_copies = [pltpu.make_async_copy(ext_hbm, ext, more[3].at[0])]
+        small.append((ext_hbm, ext))
     else:
-        first_copies = [
-            pltpu.make_async_copy(key_hbm, key_ref, more[0].at[0]),
-            pltpu.make_async_copy(value_hbm, value_ref, more[0].at[1]),
-        ]
-    for copy in first_copies:
+        query_ref, key_ref, value_ref = more
+        small += [(query_hbm, query_ref), (key_hbm, key_ref), (value_hbm, value_ref)]
+    small = [pltpu.make_async_copy(src, dst, sem.at[n]) for n, (src, dst) in enumerate(small)]
+    px_copy(0).start()
+    for copy in small:
         copy.start()
     w_copy(0).start()
-    fetch(1)
-    for copy in px_copies(2):
-        copy.start()
+    px_copy(1).start()
+    w_copy(1).start()
+    px_copy(2).start()
 
     def relayout(v, a_ref, stage):
         body = px[v].astype(F32)
         if edge:
-            groups = [more[0][v].astype(F32), body[0:8], body[8:16], body[16:24],
-                      body[40:48], body[48:56], body[56:64], more[1][v].astype(F32)]
+            groups = [low_ref[v].astype(F32), body[0:8], body[8:16], body[16:24],
+                      body[40:48], body[48:56], body[56:64], high_ref[v].astype(F32)]
         else:
             groups = [body[8 * n : 8 * n + 8] for n in range(1, 7)]
         for n, group in enumerate(groups):
             relayout_group(group, stage.at[n], edges.at[n], a_ref.at[n])
 
-    def compute(v, a_ref):
+    def embed_tokens(v, a_ref, tok):
         a = jnp.concatenate(
             [
                 jnp.concatenate([a_ref[start + g, b * TILES : b * TILES + PC, :] for g in range(4) for b in range(2)], 1)
@@ -125,9 +112,11 @@
         weight = jnp.concatenate(
             [w[v, 8 * g : 8 * g + 8, 16 * b : 16 * b + 16, :].reshape(LANES, D) for g in range(4) for b in range(2)], 0
         )
-        tokens = (jnp.dot(a, weight, preferred_element_type=F32) + off_ref[v]).astype(BF)
-        both = lax.dot_general(ext[...], tokens, NT, preferred_element_type=F32)
-        scores = both[D : D + 8] + both[D + 8 : D + 16] + both[D + 16 : D + 24] + bias_ref[v]
+        tok[...] = (jnp.dot(a, weight, preferred_element_type=F32) + off_ref[v]).astype(BF)
+
+    def attend(v, tok):
+        both = lax.dot_general(ext[...], tok[...], NT, preferred_element_type=F32)
+        scores = both[0:8] + both[8:16] + both[16:24] + bias_ref[v + 1]
         old = top_ref[...]
         top = jnp.maximum(old, scores)
         decay = jnp.exp(old - top)
@@ -136,20 +125,24 @@
         tot_ref[...] = tot_ref[...] * decay + fresh
         for h in range(HEADS):
             at = slice(h * HEAD, (h + 1) * HEAD)
-            acc_ref[at, :] = acc_ref[at, :] * decay[h : h + 1] + both[at] * fresh[h : h + 1]
+            acc_ref[at, :] = acc_ref[at, :] * decay[h : h + 1] + both[32 + h * HEAD : 32 + (h + 1) * HEAD] * fresh[h : h + 1]
 
     edges[...] = jnp.zeros_like(edges)
     perm = permutation()
+    small[0].wait()
+    small[1].wait()
     valid = jnp.concatenate([cnt_ref[v].astype(F32) for v in range(VPD)], 0).astype(BF)
     bias = jnp.log((1.0 + jnp.dot(valid, perm, preferred_element_type=F32)) / (1.0 + PATCH * PATCH))
     offsets = ve_ref[...].astype(F32)
     for v in range(VPD):
         off_ref[v] = offsets[v : v + 1]
-        bias_ref[v] = jnp.concatenate([bias[4 * v + row : 4 * v + row + 1] for row in rows], 1)
+        bias_ref[v + 1] = jnp.concatenate([bias[4 * v + row : 4 * v + row + 1] for row in rows], 1)
+    bias_ref[0] = jnp.full((1, 2 * PC), -1e30, F32)
+    tok_odd[...] = jnp.zeros_like(tok_odd)
     top_ref[...] = jnp.full_like(top_ref, -1e30)
     tot_ref[...] = jnp.zeros_like(tot_ref)
     acc_ref[...] = jnp.zeros_like(acc_ref)
-    for copy in first_copies:
+    for copy in small[2:]:
         copy.wait()
     if not edge:
         head = lax.broadcasted_iota(jnp.int32, (HEADS, D), 0)
@@ -157,11 +150,11 @@
         spread = jnp.where(col // HEAD == head, jnp.broadcast_to(query_ref[...], (HEADS, D)), 0.0)
         parts = lax.dot_general(jnp.concatenate(three_parts(spread), 0), key_ref[...], NT, preferred_element_type=F32)
         kq = (parts[0:8] + parts[8:16] + parts[16:24]) / math.sqrt(HEAD)
-        ext[0:D, :] = value_ref[...].T
-        ext[D : D + 32, :] = jnp.concatenate((*three_parts(kq), jnp.zeros((8, D), BF)), 0)
-        ext_out[...] = ext[...]
-    for copy in px_copies(0):
-        copy.wait()
+        ext[32 : D + 32, :] = value_ref[...].T
+        ext[0:32, :] = jnp.concatenate((*three_parts(kq), jnp.zeros((8, D), BF)), 0)
+        ext_copy = pltpu.make_async_copy(ext, ext_out, sem.at[0])
+        ext_copy.start()
+    px_copy(0).wait()
     relayout(0, a_even, stage_even)
 
     def pair(step, _):
@@ -171,30 +164,33 @@
         @pl.when(step < VPD // 2 - 1)
         def _():
             w_copy(even + 2).start()
-            fetch(even + 3)
+            px_copy(even + 3).start()
+            w_copy(even + 3).start()
 
         @pl.when(step < VPD // 2 - 2)
         def _():
-            for copy in px_copies(even + 4):
-                copy.start()
+            px_copy(even + 4).start()
 
         w_copy(even).wait()
         w_copy(even + 1).wait()
-        for copy in px_copies(even + 1):
-            copy.wait()
+        px_copy(even + 1).wait()
 
         @pl.when(step < VPD // 2 - 1)
         def _():
-            for copy in px_copies(even + 2):
-                copy.wait()
-
+            px_copy(even + 2).wait()
+
+        embed_tokens(even, a_even, tok_even)
+        attend(even - 1, tok_odd)
         relayout(even + 1, a_odd, stage_odd)
-        compute(even, a_even)
+        embed_tokens(even + 1, a_odd, tok_odd)
+        attend(even, tok_even)
         relayout(later, a_even, stage_even)
-        compute(even + 1, a_odd)
         return 0
 
     lax.fori_loop(0, VPD // 2, pair, 0)
+    attend(VPD - 1, tok_odd)
+    if not edge:
+        ext_copy.wait()
 
     lane = lax.broadcasted_iota(jnp.int32, (24, LANES), 1)
     total = tot_ref[...]
@@ -221,43 +217,41 @@
 
 def embed(edge, extras, pixels, weight, counts, var_embed):
     groups = 8 if edge else 6
-    hbm = pl.BlockSpec(memory_space=pl.ANY)
+    hbm = pl.BlockSpec(memory_space=pltpu.HBM)
     vmem = pl.BlockSpec(memory_space=pltpu.VMEM)
     out_shape = [jax.ShapeDtypeStruct((DEVS, 2 * OWN + 16, D), BF)]
     scratch = [
         pltpu.VMEM((VPD, 64, COLS), BF),
         pltpu.VMEM((VPD, 32, 32, D), BF),
         pltpu.VMEM((D + 32, D), BF),
+        pltpu.VMEM((VPD, 4, PC), jnp.int32),
+        pltpu.VMEM((VPD, D), BF),
         pltpu.VMEM((groups, PC + TILES, LANES), BF),
         pltpu.VMEM((groups, PC + TILES, LANES), BF),
         pltpu.VMEM((groups, TILES * 8, LANES), F32),
         pltpu.VMEM((groups, TILES * 8, LANES), F32),
         pltpu.VMEM((groups, TILES + 16, LANES), F32),
-        pltpu.VMEM((VPD, 1, 2 * PC), F32),
+        pltpu.VMEM((D, D), BF),
+        pltpu.VMEM((D, D), BF),
+        pltpu.VMEM((VPD + 1, 1, 2 * PC), F32),
         pltpu.VMEM((VPD, 1, D), F32),
         pltpu.VMEM((HEADS, 2 * PC), F32),
         pltpu.VMEM((HEADS, 2 * PC), F32),
         pltpu.VMEM((D, 2 * PC), F32),
         pltpu.SemaphoreType.DMA((VPD,)),
         pltpu.SemaphoreType.DMA((VPD,)),
+        pltpu.SemaphoreType.DMA((5,)),
     ]
-    if edge:
-        scratch += [
-            pltpu.VMEM((VPD, 8, COLS), BF),
-            pltpu.VMEM((VPD, 8, COLS), BF),
-            pltpu.SemaphoreType.DMA((2, VPD)),
-            pltpu.SemaphoreType.DMA((1,)),
-        ]
-    else:
-        scratch += [pltpu.SemaphoreType.DMA((2,)), pltpu.VMEM((D, D), BF), pltpu.VMEM((D, D), BF)]
+    if not edge:
         out_shape.append(jax.ShapeDtypeStruct((D + 32, D), BF))
+        scratch += [pltpu.VMEM((1, D), F32), pltpu.VMEM((D, D), BF), pltpu.VMEM((D, D), BF)]
     return pl.pallas_call(
         functools.partial(embed_kernel, edge),
-        in_specs=[hbm if edge else vmem, hbm, hbm, hbm, hbm, vmem, vmem],
-        out_specs=[vmem] * len(out_shape),
+        in_specs=[vmem if edge else hbm] * 2 + [hbm] * 5,
+        out_specs=[vmem, hbm][: len(out_shape)],
         out_shape=out_shape,
         scratch_shapes=scratch,
-        compiler_params=pltpu.CompilerParams(vmem_limit_bytes=56 * 2**20),
+        compiler_params=pltpu.CompilerParams(vmem_limit_bytes=(48 if edge else 56) * 2**20),
         cost_estimate=pl.CostEstimate(flops=8 * 2 * 512 * (1024 + 512) * 512, bytes_accessed=13 * 2**20, transcendentals=0),
         name="embed_edge" if edge else "embed_inner",
     )(*extras, pixels, weight, counts, var_embed)

time: 61.5 us -> 56 us (0.911)
  Pallas kernels: 30.4 us -> 25.1 us
    pallas_call x2, Pallas kernels: 28.7 us -> 23.4 us  [embed(): pl.pallas_call(functools.partial(embed_kernel, edge), in_specs=[vmem if e...]
  transfers between devices with their start and end apart: 3 -> 3, of which waited for: 0 -> 0; matrix products, arithmetic and copies ran while one was open for 0% -> 0% of each run, Pallas kernels for 47% -> 42%
where the time goes in v1:
time: 56 us; the launch traced here: 55.7 us
  Pallas kernels  25.1 us (45%)
  blocking collectives  14.9 us (27%)
  starting transfers between devices  13.3 us (24%)
  local copies, waits for them, and re-layouts  2.33 us (4%)
    pallas_call x2, Pallas kernels, embed(): pl.pallas_call(functools.partial(embed_kernel, edge), in_specs=[vmem if e...  23.4 us
    all_to_all x1, blocking collectives, exchange(): return lax.all_to_all(msg, 'var', 0, 0)  14.9 us
    ppermute x1, starting transfers between devices, shards(): high = lax.ppermute(pixels[:, 0:8], 'space', [(b, a) for a, b in forward])  6.05 us
    all_to_all x1, starting transfers between devices, exchange(): return lax.all_to_all(msg, 'var', 0, 0)  5.32 us
    ppermute x1, starting transfers between devices, shards(): low = lax.ppermute(pixels[:, 56:64], 'space', forward)  1.92 us
    pallas_call x1, Pallas kernels, finish(): pl.pallas_call(finish_kernel, out_shape=jax.ShapeDtypeStruct((4, OWN, D),...  1.74 us
    slice x1, local copies, waits for them, and re-layouts, shards(): high = lax.ppermute(pixels[:, 0:8], 'space', [(b, a) for a, b in forward])  1.27 us
  transfers between devices with their start and end apart: 3, of which 0 were waited for; matrix products, arithmetic and copies ran while one was open for 0% of the time, Pallas kernels for 42%

profile of v1, /device:TPU:96, one launch (start us, length us, event | category | flops | bytes accessed | tf_op | source)
XLA Modules:
  0.0 55.7 jit_solution(7615353862842627120)
XLA Ops:
  0.0 1.3 %fusion = (bf16[8,8,4096]{2,1,0:T(8,128)(2,1)S(1)}, bf16[8,8,4096]{2,1,0:T(8,128)(2,1)S(1)}) fusion(bf16[8,64,4096]{2,1,0:T(8,128)(2,1)} %refs_3_.3), kind=kLoop, calls=%fused_computation | loop fusion | bytes 2097152 | tf_op jit(solution)/shard_map/slice | solution.py:302
  1.3 1.9 %collective-permute-start = (bf16[8,8,4096]{2,1,0:T(8,128)(2,1)S(1)}, bf16[8,8,4096]{2,1,0:T(8,128)(2,1)S(1)}, u32[]{:S(2)}, u32[]{:S(2)}) collective-permute-start(bf16[8,8,4096]{2,1,0:T(8,128)(2,1)S(1)} %get-tuple-element.10), channel_id=1, source_target_pairs={{0,1},{1,2},{2,3},{3,4},{4,5},{5,6},{6,7},{7,8},{8,9},{9,10},{10,1... | collective-permute-start | bytes 1572872 | tf_op jit(solution)/shard_map/ppermute | solution.py:301
  3.2 6.0 %collective-permute-start.1 = (bf16[8,8,4096]{2,1,0:T(8,128)(2,1)S(1)}, bf16[8,8,4096]{2,1,0:T(8,128)(2,1)S(1)}, u32[]{:S(2)}, u32[]{:S(2)}) collective-permute-start(bf16[8,8,4096]{2,1,0:T(8,128)(2,1)S(1)} %get-tuple-element.9), channel_id=1, source_target_pairs={{1,0},{2,1},{3,2},{4,3},{5,4},{6,5},{7,6},{8,7},{9,8},{10,9},{11,1... | collective-permute-start | bytes 1572872 | tf_op jit(solution)/shard_map/ppermute | solution.py:302
  9.3 0.0 copy-start.1
  9.3 0.0 copy-start.2
  9.3 12.3 %embed_inner.1 = (bf16[8,80,512]{2,1,0:T(8,128)(2,1)}, bf16[544,512]{1,0:T(8,128)(2,1)}) custom-call(f32[1,512]{1,0:T(1,128)} %bitcast.1, bf16[512,512]{1,0:T(8,128)(2,1)} %refs_1_.1, bf16[512,512]{1,0:T(8,128)(2,1)} %refs_2_.1, bf16[8,64,4096]{2,1,0:T(8,128)(2,1)} %refs_3_.3, bf16[8,32,32,512]{3,2,1,0:T(8,128)(2,1)} %refs_4_.3, s32[8,4,256]{2,1,0:T(4,128)} %refs_5_.3, ...), custom_call_target="tpu_custom_call" | custom-call | flops 6442450944 | bytes 13631488 | tf_op jit(solution)/shard_map/embed_inner/pallas_call | solution.py:248
  21.6 5.3 %all-to-all-start = ((bf16[8,80,512]{2,1,0:T(8,128)(2,1)}), bf16[8,80,512]{2,1,0:T(8,128)(2,1)S(1)}, u32[]{:S(2)}, u32[]{:S(2)}) async-start(bf16[8,80,512]{2,1,0:T(8,128)(2,1)} %get-tuple-element.7), calls=%async_computation | async-start | bytes 1310720 | tf_op jit(solution)/shard_map/all_to_all | solution.py:295
  27.0 0.0 collective-permute-done.refs_0_
  27.0 0.0 collective-permute-done.1.refs_1_
  27.0 0.0 copy-done.1
  27.0 0.0 copy-done.2
  27.0 0.0 copy-start.3
  27.0 1.0 %copy-done.3 = bf16[544,512]{1,0:T(8,128)(2,1)S(1)} copy-done((bf16[544,512]{1,0:T(8,128)(2,1)S(1)}, bf16[544,512]{1,0:T(8,128)(2,1)}, u32[]{:S(2)}) %copy-start.3) | copy-done | bytes 557080
  28.0 0.0 copy-start
  28.0 11.0 %embed_edge.1 = bf16[8,80,512]{2,1,0:T(8,128)(2,1)S(1)} custom-call(bf16[8,8,4096]{2,1,0:T(8,128)(2,1)S(1)} %collective-permute-done.refs_0_, bf16[8,8,4096]{2,1,0:T(8,128)(2,1)S(1)} %collective-permute-done.1.refs_1_, bf16[544,512]{1,0:T(8,128)(2,1)S(1)} %copy-done.3, bf16[8,64,4096]{2,1,0:T(8,128)(2,1)} %refs_3_.3, bf16[8,32,32,512]{3,2,1,0:T(8,128)(2,1)} %refs_4_.3, ...), custom_call_target="tpu_custom_call" | custom-call | flops 6442450944 | bytes 13631488 | tf_op jit(solution)/shard_map/embed_edge/pallas_call | solution.py:248
  39.1 0.0 all-to-all-done.inner_ref
  39.1 14.9 %all_to_all.10.outer_ref = bf16[8,80,512]{2,1,0:T(8,128)(2,1)S(1)} all-to-all(bf16[8,80,512]{2,1,0:T(8,128)(2,1)S(1)} %embed_edge.1), channel_id=1, replica_groups=mesh['var'=8,'space'=16] {'var'}, dimensions={0} | all-to-all | bytes 1310720 | tf_op jit(solution)/shard_map/all_to_all | solution.py:295
  54.0 0.0 copy-done
  54.0 1.7 %finish.1 = bf16[4,32,512]{2,1,0:T(8,128)(2,1)} custom-call(bf16[8,80,512]{2,1,0:T(8,128)(2,1)S(1)} %all-to-all-done.inner_ref, bf16[8,80,512]{2,1,0:T(8,128)(2,1)S(1)} %all_to_all.10.outer_ref, bf16[512,512]{1,0:T(8,128)(2,1)S(1)} %copy-done), custom_call_target="tpu_custom_call" | custom-call | tf_op jit(solution)/shard_map/finish/pallas_call | solution.py:286
Async XLA Ops:
  1.3 25.7 %collective-permute-start = (bf16[8,8,4096]{2,1,0:T(8,128)(2,1)S(1)}, bf16[8,8,4096]{2,1,0:T(8,128)(2,1)S(1)}, u32[]{:S(2)}, u32[]{:S(2)}) collective-permute-start(bf16[8,8,4096]{2,1,0:T(8,128)(2,1)S(1)} %get-tuple-element.10), channel_id=1, source_target_pairs={{0,1},{1,2},{2,3},{3,4},{4,5},{5,6},{6,7},{7,8},{8,9},{9,10},{10,1... | collective-permute-start | bytes 1572872 | tf_op jit(solution)/shard_map/ppermute | solution.py:301
  3.2 23.8 %collective-permute-start.1 = (bf16[8,8,4096]{2,1,0:T(8,128)(2,1)S(1)}, bf16[8,8,4096]{2,1,0:T(8,128)(2,1)S(1)}, u32[]{:S(2)}, u32[]{:S(2)}) collective-permute-start(bf16[8,8,4096]{2,1,0:T(8,128)(2,1)S(1)} %get-tuple-element.9), channel_id=1, source_target_pairs={{1,0},{2,1},{3,2},{4,3},{5,4},{6,5},{7,6},{8,7},{9,8},{10,9},{11,1... | collective-permute-start | bytes 1572872 | tf_op jit(solution)/shard_map/ppermute | solution.py:302
  9.3 17.7 %copy-start.1 = (s32[8,4,256]{2,1,0:T(4,128)S(1)}, s32[8,4,256]{2,1,0:T(4,128)}, u32[]{:S(2)}) copy-start(s32[8,4,256]{2,1,0:T(4,128)} %refs_5_.3) | copy-start | bytes 98308
  9.3 17.7 %copy-start.2 = (bf16[8,512]{1,0:T(8,128)(2,1)S(1)}, bf16[8,512]{1,0:T(8,128)(2,1)}, u32[]{:S(2)}) copy-start(bf16[8,512]{1,0:T(8,128)(2,1)} %refs_6_.3) | copy-start | bytes 24580
  21.6 17.4 %all-to-all-start = ((bf16[8,80,512]{2,1,0:T(8,128)(2,1)}), bf16[8,80,512]{2,1,0:T(8,128)(2,1)S(1)}, u32[]{:S(2)}, u32[]{:S(2)}) async-start(bf16[8,80,512]{2,1,0:T(8,128)(2,1)} %get-tuple-element.7), calls=%async_computation | async-start | bytes 1310720 | tf_op jit(solution)/shard_map/all_to_all | solution.py:295
  27.0 1.1 %copy-start.3 = (bf16[544,512]{1,0:T(8,128)(2,1)S(1)}, bf16[544,512]{1,0:T(8,128)(2,1)}, u32[]{:S(2)}) copy-start(bf16[544,512]{1,0:T(8,128)(2,1)} %get-tuple-element.8.refs_2_) | copy-start | bytes 1671172
  28.0 25.9 %copy-start = (bf16[512,512]{1,0:T(8,128)(2,1)S(1)}, bf16[512,512]{1,0:T(8,128)(2,1)}, u32[]{:S(2)}) copy-start(bf16[512,512]{1,0:T(8,128)(2,1)} %wo_ref.1) | copy-start | bytes 1572868
